TPU v7x, 256 devices: a whole 4x4x8 slice. The times are simulated.
256 devices in a mesh: row: 32 (over z_hi, y, x), col: 8 (over z_lo, core).
Axes of the slice: x: 4, y: 4, z: 8 (z_hi: 2, z_lo: 4; z = z_hi * 4 + z_lo), core: 2. Of those that a mesh axis runs over, the one named last changes fastest.
Arguments:
- counts: int32 [8192, 8192], P('row', 'col'), may hold values from 0 to 63
- inverse_capacity: float32 [8192, 8192], P('row', 'col'), may hold values from 0.25 to 2, as said below
Outputs:
- field_first: float32 [8192, 8192], P('row', 'col')
- field_second: float32 [8192, 8192], P('row', 'col')
Inputs may be any that keep to these rules, and one draw needn't show every extreme that they name: `inverse_capacity`: positive.
All inputs are finite; a program needn't handle non-finite values.
Results may differ from a plain program's by a relative error of at most 0.002.
Values sent between devices are 32-bit elements; how exact they have to be, the bound alone decides.
A program may use at most 64 MiB of HBM per device.

v0:
```python
import math

import jax
import jax.numpy as jnp
from jax import lax
from jax.sharding import PartitionSpec as P

HIGHEST = lax.Precision.HIGHEST


def split_sizes(length):
    fine_size = min(128, length)
    return (length // fine_size, fine_size)


def scrambled_index(positions, length):
    coarse_size, fine_size = split_sizes(length)
    return positions // fine_size + coarse_size * (positions % fine_size)


def circle_tables(length, rotation):
    positions = jnp.arange(length, dtype=jnp.int32)
    product = positions[:, None] * positions[None, :] % length
    angles = product.astype(jnp.float32) * (2.0 * math.pi / length)
    return (jnp.cos(angles), rotation * jnp.sin(angles))


def twist_tables(coarse_size, fine_size, rotation):
    length = coarse_size * fine_size
    product = (
        jnp.arange(coarse_size, dtype=jnp.int32)[:, None]
        * jnp.arange(fine_size, dtype=jnp.int32)[None, :]
        % length
    )
    angles = product.astype(jnp.float32) * (2.0 * math.pi / length)
    return (jnp.cos(angles), rotation * jnp.sin(angles))


def half_phases(coarse_size, fine_size):
    length = coarse_size * fine_size
    spectral_index = (
        jnp.arange(coarse_size, dtype=jnp.int32)[:, None]
        + coarse_size * jnp.arange(fine_size, dtype=jnp.int32)[None, :]
    )
    phases = spectral_index.astype(jnp.float32) * (math.pi / (2.0 * length))
    return (jnp.cos(phases), jnp.sin(phases))


def mixing_matrix(fine_size, rotation):
    cosine_part, sine_part = circle_tables(fine_size, rotation)
    upper_part = jnp.concatenate([cosine_part, sine_part], axis=1)
    lower_part = jnp.concatenate([-sine_part, cosine_part], axis=1)
    return jnp.concatenate([upper_part, lower_part], axis=0)


def fourier_forward(signal):
    height, length = signal.shape
    coarse_size, fine_size = split_sizes(length)
    blocked = signal.reshape(height, coarse_size, fine_size)
    coarse_cos, coarse_sin = circle_tables(coarse_size, -1.0)
    section_one = jnp.einsum(
        "hab,ka->hkb", blocked, jnp.concatenate([coarse_cos, coarse_sin], axis=0), precision=HIGHEST
    )
    real_one = section_one[:, :coarse_size]
    imag_one = section_one[:, coarse_size:]
    twist_cos, twist_sin = twist_tables(coarse_size, fine_size, -1.0)
    real_two = real_one * twist_cos - imag_one * twist_sin
    imag_two = real_one * twist_sin + imag_one * twist_cos
    joined = jnp.concatenate([real_two, imag_two], axis=2).reshape(
        height * coarse_size, 2 * fine_size
    )
    result = jnp.dot(
        joined,
        mixing_matrix(fine_size, -1.0),
        precision=HIGHEST,
        preferred_element_type=jnp.float32,
    )
    result = result.reshape(height, coarse_size, 2 * fine_size)
    return (result[:, :, :fine_size], result[:, :, fine_size:])


def cosine_forward(matrix):
    height, length = matrix.shape
    folded = jnp.concatenate([matrix[:, 0::2], jnp.flip(matrix[:, 1::2], axis=1)], axis=1)
    real_part, imag_part = fourier_forward(folded)
    coarse_size, fine_size = split_sizes(length)
    phase_cos, phase_sin = half_phases(coarse_size, fine_size)
    return (real_part * phase_cos + imag_part * phase_sin).reshape(height, length)


def partner_of(blocked):
    height = blocked.shape[0]
    lower_part = jnp.flip(blocked[:, 1:, :], axis=(1, 2))
    upper_part = jnp.concatenate(
        [jnp.zeros((height, 1, 1), blocked.dtype), jnp.flip(blocked[:, :1, 1:], axis=2)], axis=2
    )
    return jnp.concatenate([upper_part, lower_part], axis=1)


def corner_mask(coarse_size, fine_size):
    top_row = jnp.arange(coarse_size, dtype=jnp.int32)[:, None] == 0
    left_column = jnp.arange(fine_size, dtype=jnp.int32)[None, :] == 0
    return (top_row & left_column).astype(jnp.float32)


def fourier_inverse_fold(leading, partner):
    height, coarse_size, fine_size = leading.shape
    length = coarse_size * fine_size
    phase_cos, phase_sin = half_phases(coarse_size, fine_size)
    real_part = phase_cos * leading + phase_sin * partner
    imag_part = phase_sin * leading - phase_cos * partner
    joined = jnp.concatenate([real_part, imag_part], axis=2).reshape(
        height * coarse_size, 2 * fine_size
    )
    result = jnp.dot(
        joined, mixing_matrix(fine_size, 1.0), precision=HIGHEST, preferred_element_type=jnp.float32
    )
    result = result.reshape(height, coarse_size, 2 * fine_size)
    real_one = result[:, :, :fine_size]
    imag_one = result[:, :, fine_size:]
    twist_cos, twist_sin = twist_tables(coarse_size, fine_size, 1.0)
    real_two = real_one * twist_cos - imag_one * twist_sin
    imag_two = real_one * twist_sin + imag_one * twist_cos
    coarse_cos, coarse_sin = circle_tables(coarse_size, 1.0)
    stacked = jnp.concatenate([real_two, imag_two], axis=1)
    combiner = jnp.concatenate([coarse_cos, -coarse_sin], axis=1)
    folded = (
        jnp.einsum("hkb,ak->hab", stacked, combiner, precision=HIGHEST).reshape(height, length)
        * 0.5
    )
    midpoint = length // 2
    even_part = folded[:, :midpoint]
    odd_part = jnp.flip(folded[:, midpoint:], axis=1)
    return jnp.stack([even_part, odd_part], axis=2).reshape(height, length)


def cosine_sum(matrix):
    height, length = matrix.shape
    coarse_size, fine_size = split_sizes(length)
    blocked = matrix.reshape(height, coarse_size, fine_size)
    corner = corner_mask(coarse_size, fine_size)
    return fourier_inverse_fold(blocked * (1.0 + corner), partner_of(blocked))


def sine_sum(matrix):
    height, length = matrix.shape
    coarse_size, fine_size = split_sizes(length)
    blocked = matrix.reshape(height, coarse_size, fine_size)
    corner = corner_mask(coarse_size, fine_size)
    result = fourier_inverse_fold(partner_of(blocked), blocked * (1.0 - corner))
    parity = 1.0 - 2.0 * (jnp.arange(length, dtype=jnp.int32) % 2).astype(jnp.float32)
    return result * parity[None, :]


def spectral_weight(omega_down, omega_across):
    denominator = omega_down * omega_down + omega_across * omega_across
    corner = (omega_down == 0.0) & (omega_across == 0.0)
    return jnp.where(corner, 0.0, 1.0 / jnp.where(corner, 1.0, denominator))


def to_row_pencils(stacked):
    turned = jnp.swapaxes(stacked, 1, 2)
    return lax.all_to_all(turned, "row", split_axis=1, concat_axis=2, tiled=True)


def from_row_pencils(stacked):
    arrived = lax.all_to_all(stacked, "row", split_axis=2, concat_axis=1, tiled=True)
    return jnp.swapaxes(arrived, 1, 2)


def to_col_pencils(stacked):
    return lax.all_to_all(stacked, "col", split_axis=1, concat_axis=2, tiled=True)


def from_col_pencils(stacked):
    return lax.all_to_all(stacked, "col", split_axis=2, concat_axis=1, tiled=True)


def on_device(counts, inverse_capacity):
    row_count = lax.axis_size("row")
    col_count = lax.axis_size("col")
    row_place = lax.axis_index("row")
    col_place = lax.axis_index("col")
    height, breadth = counts.shape
    size_down = height * row_count
    size_across = breadth * col_count
    norming = 4.0 / math.sqrt(size_down * size_across)
    density = counts.astype(jnp.float32) * inverse_capacity * 0.03125
    along_down = cosine_forward(to_row_pencils(density[None])[0])
    spectral_rows = to_col_pencils(from_row_pencils(along_down[None]))[0]
    coefficients = cosine_forward(spectral_rows) * norming
    local_rows = coefficients.shape[0]
    row_positions = (
        row_place * height + col_place * local_rows + jnp.arange(local_rows, dtype=jnp.int32)
    )
    omega_down = math.pi * scrambled_index(row_positions, size_down).astype(jnp.float32)
    omega_across = math.pi * scrambled_index(
        jnp.arange(size_across, dtype=jnp.int32), size_across
    ).astype(jnp.float32)
    spectral = coefficients * spectral_weight(omega_down[:, None], omega_across[None, :])
    inverse_pair = jnp.stack([cosine_sum(spectral), sine_sum(spectral * omega_across[None, :])])
    arrived = to_row_pencils(from_col_pencils(inverse_pair))
    omega_last = math.pi * scrambled_index(
        jnp.arange(size_down, dtype=jnp.int32), size_down
    ).astype(jnp.float32)
    fields = jnp.stack([sine_sum(arrived[0] * omega_last[None, :]), cosine_sum(arrived[1])])
    result = from_row_pencils(fields)
    return (result[0], result[1])


def solution(mesh):
    return jax.shard_map(
        on_device,
        mesh=mesh,
        in_specs=(P("row", "col"), P("row", "col")),
        out_specs=(P("row", "col"), P("row", "col")),
        check_vma=False,
    )
```

profile of v0, /device:TPU:1, one launch (start us, length us, event | category | flops | bytes accessed | tf_op | source)
XLA Modules:
  0.0 641.2 jit_solution(4548431401881595729)
XLA Ops:
  4.5 14.5 %all-to-all-start = ((f32[1,1024,256]{2,0,1:T(1,128)}), f32[1,1024,256]{2,0,1:T(1,128)S(1)}, u32[]{:S(2)}, u32[]{:S(2)}) async-start(f32[1,1024,256]{2,0,1:T(1,128)} %reshape_bitcast_fusion), calls=%async_computation | async-start | bytes 2097152 | tf_op jit(solution)/shard_map/all_to_all | solution.py:163
  20.0 19.9 %all-to-all-done = f32[1,1024,256]{2,0,1:T(1,128)S(1)} async-done(((f32[1,1024,256]{2,0,1:T(1,128)}), f32[1,1024,256]{2,0,1:T(1,128)S(1)}, u32[]{:S(2)}, u32[]{:S(2)}) %all-to-all-start) | async-done | bytes 1048608 | tf_op jit(solution)/shard_map/all_to_all | solution.py:163
  40.1 17.6 %slice.123 = f32[32,4096]{1,0:T(8,128)S(1)} slice(f32[32,8192]{1,0:T(8,128)S(1)} %bitcast.155), slice={[0:32:1], [1:8192:2]} | slice | bytes 1048576 | tf_op jit(solution)/shard_map/slice | solution.py:84
  57.7 17.6 %slice.122 = f32[32,4096]{1,0:T(8,128)S(1)} slice(f32[32,8192]{1,0:T(8,128)S(1)} %bitcast.156), slice={[0:32:1], [0:8192:2]} | slice | bytes 1048576 | tf_op jit(solution)/shard_map/slice | solution.py:84
  85.8 38.5 %reduce = f32[8192,32]{1,0:T(8,128)} reduce(f32[8192,1,32]{2,1,0:T(1,128)} %bitcast.137, f32[]{:T(128)} %broadcast.803), dimensions={1}, to_apply=%bitcast.115.reduce_sub_computation | reduce | bytes 2097156
  128.1 20.0 %all_to_all.99 = f32[32,1,8192]{2,1,0:T(1,128)S(1)} all-to-all(f32[32,1,8192]{2,1,0:T(1,128)S(1)} %reshape.486), channel_id=1, replica_groups=mesh['row'=32,'col'=8] {'row'}, dimensions={0} | all-to-all | bytes 2097152 | tf_op jit(solution)/shard_map/all_to_all | solution.py:167
  151.4 8.3 %reshape.487 = f32[8192,1,32]{2,1,0:T(1,128)} reshape(f32[32,8192]{1,0:T(8,128)S(1)} %reduce.1) | data formatting | bytes 2097152
  165.3 21.9 %all-to-all-start.2 = ((f32[1,256,1024]{2,0,1:T(1,128)}), f32[1,256,1024]{2,0,1:T(1,128)S(1)}, u32[]{:S(2)}, u32[]{:S(2)}) async-start(f32[1,256,1024]{2,0,1:T(1,128)} %copy.126), calls=%async_computation.2 | async-start | bytes 2097152 | tf_op jit(solution)/shard_map/all_to_all | solution.py:172
  189.8 23.1 %all-to-all-done.2 = f32[1,256,1024]{2,0,1:T(1,128)S(1)} async-done(((f32[1,256,1024]{2,0,1:T(1,128)}), f32[1,256,1024]{2,0,1:T(1,128)S(1)}, u32[]{:S(2)}, u32[]{:S(2)}) %all-to-all-start.2) | async-done | bytes 1048608 | tf_op jit(solution)/shard_map/all_to_all | solution.py:172
  213.1 17.6 %slice.129 = f32[32,4096]{1,0:T(8,128)S(1)} slice(f32[32,8192]{1,0:T(8,128)S(1)} %bitcast.157), slice={[0:32:1], [1:8192:2]} | slice | bytes 1048576 | tf_op jit(solution)/shard_map/slice | solution.py:84
  230.7 17.6 %slice.128 = f32[32,4096]{1,0:T(8,128)S(1)} slice(f32[32,8192]{1,0:T(8,128)S(1)} %bitcast.158), slice={[0:32:1], [0:8192:2]} | slice | bytes 1048576 | tf_op jit(solution)/shard_map/slice | solution.py:84
  295.4 31.8 %copy.185 = f32[2,32,8192]{1,0,2:T(2,128)} copy(f32[2,32,8192]{1,2,0:T(8,128)S(1)} %pad_maximum_fusion) | data formatting | bytes 4194304 | tf_op jit(solution)/shard_map/stack | solution.py:201
  327.2 10.3 %reshape.488 = f32[8,1,65536]{2,1,0:T(1,128)S(1)} reshape(f32[8192,2,32]{2,1,0:T(2,128)} %bitcast.133) | data formatting | bytes 4194304
  337.5 52.0 %all_to_all.100 = f32[8,1,65536]{2,1,0:T(1,128)} all-to-all(f32[8,1,65536]{2,1,0:T(1,128)S(1)} %reshape.488), channel_id=1, replica_groups=mesh['row'=32,'col'=8] {'col'}, dimensions={0} | all-to-all | bytes 4194304 | tf_op jit(solution)/shard_map/all_to_all | solution.py:176
  389.6 7.3 %reduce.2 = f32[8,65536]{1,0:T(8,128)S(1)} reduce(f32[8,1,65536]{2,1,0:T(1,128)} %all_to_all.100, f32[]{:T(128)} %broadcast.803), dimensions={1}, to_apply=%all_to_all.82.reduce_sub_computation | reduce | bytes 4194308 | tf_op jit(solution)/shard_map/all_to_all | solution.py:176
  396.9 10.3 %reshape.489 = f32[8192,2,32]{2,1,0:T(2,128)} reshape(f32[8,65536]{1,0:T(8,128)S(1)} %reduce.2) | data formatting | bytes 4194304
  407.2 10.2 %copy.158 = f32[2,32,8,1024]{3,1,2,0:T(8,128)S(1)} copy(f32[2,32,8,1024]{1,0,3,2:T(2,128)} %bitcast.131) | data formatting | bytes 4194304 | tf_op jit(solution)/shard_map/all_to_all | solution.py:176
  419.7 53.7 %all_to_all.101 = f32[2,1024,256]{2,0,1:T(2,128)S(1)} all-to-all(f32[2,1024,256]{2,0,1:T(2,128)} %copy.135), channel_id=1, replica_groups=mesh['row'=32,'col'=8] {'row'}, dimensions={1} | all-to-all | bytes 4194304 | tf_op jit(solution)/shard_map/all_to_all | solution.py:163
  519.9 31.4 %copy.184 = f32[2,32,8192]{1,0,2:T(2,128)} copy(f32[2,32,8192]{1,2,0:T(8,128)S(1)} %pad_maximum_fusion.1) | data formatting | bytes 4194304 | tf_op jit(solution)/shard_map/stack | solution.py:206
  551.3 10.2 %reshape.490 = f32[32,1,16384]{2,1,0:T(1,128)S(1)} reshape(f32[8192,2,32]{2,1,0:T(2,128)} %bitcast.134) | data formatting | bytes 4194304
  561.4 48.7 %all_to_all.102 = f32[32,1,16384]{2,1,0:T(1,128)} all-to-all(f32[32,1,16384]{2,1,0:T(1,128)S(1)} %reshape.490), channel_id=1, replica_groups=mesh['row'=32,'col'=8] {'row'}, dimensions={0} | all-to-all | bytes 4194304 | tf_op jit(solution)/shard_map/all_to_all | solution.py:167
  610.2 7.4 %reduce.3 = f32[32,16384]{1,0:T(8,128)S(1)} reduce(f32[32,1,16384]{2,1,0:T(1,128)} %all_to_all.102, f32[]{:T(128)} %broadcast.803), dimensions={1}, to_apply=%all_to_all.89.reduce_sub_computation | reduce | bytes 4194308 | tf_op jit(solution)/shard_map/all_to_all | solution.py:167
  617.6 8.5 %reshape.491 = f32[8192,2,32]{2,1,0:T(2,128)} reshape(f32[32,16384]{1,0:T(8,128)S(1)} %reduce.3) | data formatting | bytes 4194304
  626.1 9.7 %copy.161 = f32[2,32,32,256]{3,1,2,0:T(8,128)S(1)} copy(f32[2,32,32,256]{1,0,3,2:T(2,128)} %bitcast.132) | data formatting | bytes 4194304 | tf_op jit(solution)/shard_map/all_to_all | solution.py:167
  (129 shorter events, 131.4 us)
Async XLA Ops:
  0.6 1.7 copy-start.5
  4.5 35.5 %all-to-all-start = ((f32[1,1024,256]{2,0,1:T(1,128)}), f32[1,1024,256]{2,0,1:T(1,128)S(1)}, u32[]{:S(2)}, u32[]{:S(2)}) async-start(f32[1,1024,256]{2,0,1:T(1,128)} %reshape_bitcast_fusion), calls=%async_computation | async-start | bytes 2097152 | tf_op jit(solution)/shard_map/all_to_all | solution.py:163
  165.3 47.6 %all-to-all-start.2 = ((f32[1,256,1024]{2,0,1:T(1,128)}), f32[1,256,1024]{2,0,1:T(1,128)S(1)}, u32[]{:S(2)}, u32[]{:S(2)}) async-start(f32[1,256,1024]{2,0,1:T(1,128)} %copy.126), calls=%async_computation.2 | async-start | bytes 2097152 | tf_op jit(solution)/shard_map/all_to_all | solution.py:172
  262.4 2.8 copy-start.3
  268.9 1.8 copy-start.8
  280.8 4.4 copy-start.4
  285.3 4.4 copy-start.6
  289.7 5.1 copy-start
  475.4 1.2 copy-start.1
  482.9 4.9 copy-start.2
  491.5 1.8 copy-start.9
  502.6 4.4 copy-start.7
where the time goes:
time: 654 us; the launch traced here: 641 us
  local copies, waits for them, and re-layouts  284 us (43%)
  blocking collectives  174 us (27%)
  other arithmetic  81.5 us (12%)
  waiting for transfers between devices  43 us (7%)
  starting transfers between devices  36.4 us (6%)
  matrix products  19.7 us (3%)
    all_to_all x2, blocking collectives, from_row_pencils(): lax.all_to_all(stacked, 'row', split_axis=2, concat_axis=1, tiled=True)  68.7 us
    unnamed x41, local copies, waits for them, and re-layouts  61.5 us
    all_to_all x1, blocking collectives, to_row_pencils(): lax.all_to_all(turned, 'row', split_axis=1, concat_axis=2, tiled=True)  53.7 us
    all_to_all x1, blocking collectives, from_col_pencils(): lax.all_to_all(stacked, 'col', split_axis=2, concat_axis=1, tiled=True)  52 us
    unnamed x3, other arithmetic  38.6 us
    slice x2, local copies, waits for them, and re-layouts, cosine_forward(): matrix[:, 0::2]  35.2 us
    slice x2, local copies, waits for them, and re-layouts, cosine_forward(): matrix[:, 1::2]  35.2 us
    another operation x1, local copies, waits for them, and re-layouts, on_device(): jnp.stack([cosine_sum(spectral), sine_sum(spectral * omega_across[None, :...  31.8 us
  transfers between devices with their start and end apart: 2, of which 2 were waited for; matrix products, arithmetic and copies ran while one was open for 1% of the time, Pallas kernels for 0%

commit v1 on v0

v1 whole, which is shorter than its diff:
```python
import math

import jax
import jax.numpy as jnp
import ml_dtypes
import numpy as np
from jax import lax
from jax.experimental import pallas as pl
from jax.experimental.pallas import tpu as pltpu
from jax.sharding import PartitionSpec as P

MESH = pl.DeviceIdType.MESH
F32 = jnp.float32
BF16 = jnp.bfloat16
ROWS, COLS = 32, 8
DEVICES = ROWS * COLS
LANES = 128
YA, YB = 64, 128
XA, XB = 256, 32
BINS = 8192


def tables(coarse, fine):
    half = fine // 2
    k = np.arange(coarse)[:, None]
    a = np.arange(coarse)[None, :]
    angle = np.pi * (k * a % (2 * coarse)) / coarse
    first = np.concatenate([np.cos(angle), np.sin(angle)], axis=0)
    first[coarse] = 1.0 - 2.0 * (np.arange(coarse) % 2)
    odd = 2 * np.arange(fine)[None, :] + 1
    turn = np.pi * k * odd / (2 * coarse * fine)
    m = np.arange(half)[:, None]
    low = np.pi * (m * odd % (2 * fine)) / fine
    high = np.pi * ((m + 1) * odd % (2 * fine)) / fine
    middle = np.pi * ((2 * m + 1) * odd % (4 * fine)) / (2 * fine)
    zero = np.zeros_like(low)
    cosine = np.block([[np.cos(low), -np.sin(low)], [np.cos(high), np.sin(high)]])
    cosine_top = np.block([[np.cos(low), zero], [zero, np.cos(middle)]])
    sine = np.block([[np.sin(low), np.cos(low)], [np.sin(high), -np.cos(high)]])
    sine_top = np.block([[np.sin(low), zero], [zero, np.sin(middle)]])
    place = np.arange(fine)[None, :]
    index = np.where(place < half, k + 2 * coarse * place, 2 * coarse * (place - half + 1) - k)
    index[0] = np.where(place[0] < half, 2 * coarse * place[0], coarse + 2 * coarse * (place[0] - half))
    return first, turn, cosine, cosine_top, sine, sine_top, index


def spread(matrix, copies):
    size = matrix.shape[0]
    left = np.kron(np.eye(copies), matrix[:, :size])
    right = np.kron(np.eye(copies), matrix[:, size:])
    return np.concatenate([left, right], axis=1)


def parts(matrix):
    high = matrix.astype(np.float32).astype(ml_dtypes.bfloat16)
    low = (matrix - high.astype(np.float64)).astype(np.float32).astype(ml_dtypes.bfloat16)
    return [high, low]


def constants():
    first, turn, cosine, cosine_top, sine, sine_top, _ = tables(YA, YB)
    out = []
    high, low = parts(first)
    out += [np.concatenate([high, high, low], axis=1)]
    high, low = parts(first.T)
    out += [np.concatenate([high, high, low], axis=1)]
    out += [np.cos(turn).astype(np.float32), np.sin(turn).astype(np.float32)]
    out += parts(cosine.T) + parts(cosine_top.T)
    out += parts(cosine) + parts(cosine_top) + parts(sine) + parts(sine_top)
    first, turn, cosine, cosine_top, sine, sine_top, index = tables(XA, XB)
    copies = LANES // XB
    cosine, cosine_top, sine, sine_top = (spread(t, copies) for t in (cosine, cosine_top, sine, sine_top))
    out += parts(first) + parts(first.T)
    out += [np.tile(t, (1, copies)).astype(np.float32) for t in (np.cos(turn), np.sin(turn), index)]
    out += parts(cosine.T) + parts(cosine_top.T)
    out += parts(cosine) + parts(cosine_top) + parts(sine) + parts(sine_top)
    return out


def split(x):
    high = x.astype(BF16)
    return high, (x - high.astype(F32)).astype(BF16)


def dot(x, y):
    return jnp.dot(x, y, preferred_element_type=F32)


def times_table(x, table):
    high, low = split(x)
    t_high, t_low = table[0][...], table[1][...]
    return dot(high, t_high) + dot(low, t_high) + dot(high, t_low)


def table_times(table, x):
    high, low = split(x)
    t_high, t_low = table[0][...], table[1][...]
    return dot(t_high, high) + dot(t_high, low) + dot(t_low, high)


def kernel(*refs):
    counts, inverse = refs[:2]
    c = refs[2:-21]
    (
        out_first, out_second, density, buf, bc, bs, turned, send_x, recv_x, spec, spec_top, sum_top,
        send_y, recv_y, send_b, local_sem, sends, recv_sem_rows, recv_sem_x, recv_sem_y, recv_sem_b,
    ) = refs[-21:]
    y_first, y_first_t, y_cos, y_sin = c[0:4]
    y_second, y_second_top = c[4:6], c[6:8]
    y_sum = [c[8:10], c[12:14]]
    y_sum_top = [c[10:12], c[14:16]]
    x_first, x_first_t = c[16:18], c[18:20]
    x_cos, x_sin, x_index = c[20:23]
    x_second, x_second_top = c[23:25], c[25:27]
    x_sum = [c[31:33], c[27:29]]
    x_sum_top = [c[33:35], c[29:31]]
    outs = [out_first, out_second]

    row = lax.axis_index("row")
    col = lax.axis_index("col")
    me = row * COLS + col

    def place(device):
        return (device // COLS, device % COLS)

    def remote(src, dst, send, recv, device):
        return pltpu.make_async_remote_copy(
            src_ref=src, dst_ref=dst, send_sem=send, recv_sem=recv, device_id=device, device_id_type=MESH
        )

    barrier = pltpu.get_barrier_semaphore()

    def greet(j, _):
        pl.semaphore_signal(barrier, inc=1, device_id=place(lax.rem(me + j, DEVICES)), device_id_type=MESH)
        return 0

    lax.fori_loop(1, DEVICES, greet, 0)

    def make_density(t, _):
        owner, q = t // 4, t % 4
        at = pl.multiple_of(t * 8, 8)
        values = counts[pl.ds(at, 8), :].astype(F32) * inverse[pl.ds(at, 8), :] * 0.03125
        for tile in range(8):
            density[pl.ds(pl.multiple_of(t * 64 + tile * 8, 8), 8), :] = values[:, tile * LANES:(tile + 1) * LANES]
        return 0

    lax.fori_loop(0, 32, make_density, 0)
    pl.semaphore_wait(barrier, DEVICES - 1)

    def chunk(ref, at, size):
        return ref.at[pl.ds(pl.multiple_of(at, 8), size), :]

    own = []
    for q in range(4):
        copy = pltpu.make_async_copy(chunk(density, col * 256 + q * 64, 64), chunk(buf, q * 512 + col * 64, 64), local_sem.at[q])
        copy.start()
        own.append(copy)
        for j in range(1, COLS):
            other = lax.rem(col + j, COLS)
            remote(
                chunk(density, other * 256 + q * 64, 64), chunk(buf, q * 512 + col * 64, 64),
                sends.at[0], recv_sem_rows.at[q], (row, other),
            ).start()

    neighbour = (row, lax.rem(col + 1, COLS))

    for q in range(4):
        own[q].wait()
        whole = chunk(buf, 0, (COLS - 1) * 64)
        remote(whole, whole, sends.at[0], recv_sem_rows.at[q], neighbour).wait_recv()

        def first_y(p, _):
            at = q * 512 + 2 * p
            pair = jnp.concatenate(
                [buf[pl.ds(at, YA, stride=8), :], buf[pl.ds(at + 1, YA, stride=8), :]], axis=1
            )
            high, low = split(pair)
            result = dot(y_first[...], jnp.concatenate([high, low, high], axis=0))
            for e in range(2):
                i = q * 8 + 2 * p + e
                ac = result[:YA, e * LANES:(e + 1) * LANES]
                as_ = result[YA:, e * LANES:(e + 1) * LANES]
                bc[pl.ds(i, YA, stride=32), :] = ac * y_cos[...] - as_ * y_sin[...]
                bs[pl.ds(i, YA, stride=32), :] = ac * y_sin[...] + as_ * y_cos[...]
            return 0

        lax.fori_loop(0, 4, first_y, 0)

    def second_y(t, _):
        g = lax.rem(me // 16 + t, 16)
        at = pl.multiple_of(g * LANES, LANES)
        both = jnp.concatenate([bc[pl.ds(at, LANES), :], bs[pl.ds(at, LANES), :]], axis=1)
        turned[...] = times_table(both, y_second)

        @pl.when(g == 0)
        def _():
            turned[:32, :] = times_table(both[:32], y_second_top)

        send_x[pl.ds(at, LANES), :] = turned[...].T
        return 0

    lax.fori_loop(0, 16, second_y, 0)

    own = pltpu.make_async_copy(chunk(send_x, me * 8, 8), chunk(recv_x, me * 8, 8), local_sem.at[4])
    own.start()

    def send_tiles(src, dst, send, recv):
        def step(j, _):
            other = lax.rem(me + j, DEVICES)
            remote(chunk(src, other * 8, 8), chunk(dst, me * 8, 8), send, recv, place(other)).start()
            return 0

        lax.fori_loop(1, DEVICES, step, 0)

    most = (DEVICES - 1) * 8
    send_tiles(send_x, recv_x, sends.at[1], recv_sem_x)
    own.wait()
    remote(chunk(send_x, 0, most), chunk(recv_x, 0, most), sends.at[1], recv_sem_x, neighbour).wait_recv()

    def first_x(p, _):
        pair = jnp.concatenate(
            [recv_x[pl.ds(2 * p, XA, stride=8), :], recv_x[pl.ds(2 * p + 1, XA, stride=8), :]], axis=1
        )
        result = table_times(x_first, pair)
        for e in range(2):
            s = 2 * p + e
            ac = result[:XA, e * LANES:(e + 1) * LANES]
            as_ = result[XA:, e * LANES:(e + 1) * LANES]
            both = jnp.concatenate(
                [ac * x_cos[...] - as_ * x_sin[...], ac * x_sin[...] + as_ * x_cos[...]], axis=1
            )
            spec[pl.ds(pl.multiple_of(s * XA, XA), XA), :] = times_table(both, x_second)
            spec_top[pl.ds(s, 1), :] = both[:1]
        return 0

    lax.fori_loop(0, 4, first_x, 0)
    spec[pl.ds(0, 8, stride=XA), :] = times_table(spec_top[...], x_second_top)

    norming = 4.0 / math.sqrt(BINS * BINS) / math.pi

    def v_of(step, shape):
        lane = lax.broadcasted_iota(jnp.int32, shape, 1)
        k = 4 * (me // 16) + lane // XB
        l = 8 * lax.rem(me, 16) + step
        v_low = k + 2 * YA * l
        v_high = jnp.where(k == 0, 2 * YA * (l - YB // 2) + YA, 2 * YA * (l - YB // 2 + 1) - k)
        return jnp.where(l < YB // 2, v_low, v_high).astype(F32)

    def weigh(s, _):
        at = pl.multiple_of(s * XA, XA)
        v_row = v_of(s, (1, LANES))
        u = x_index[...]
        square = u * u + v_row * v_row
        corner = square == 0.0
        weight = jnp.where(corner, 0.0, norming / jnp.where(corner, 1.0, square))
        spec[pl.ds(at, XA), :] = spec[pl.ds(at, XA), :] * weight
        return 0

    lax.fori_loop(0, 8, weigh, 0)
    top = spec[pl.ds(0, 8, stride=XA), :]
    sum_top[0] = times_table(top * x_index[:1, :], x_sum_top[0])
    sum_top[1] = times_table(top * v_of(lax.broadcasted_iota(jnp.int32, (8, LANES), 0), (8, LANES)), x_sum_top[1])
    row_of = lax.broadcasted_iota(jnp.int32, (8, 2 * LANES), 0)

    own = []
    for f in range(2):

        def sum_x(p, _):
            halves = []
            for e in range(2):
                s = 2 * p + e
                value = spec[pl.ds(pl.multiple_of(s * XA, XA), XA), :]
                factor = x_index[...] if f == 0 else v_of(s, (1, LANES))
                result = times_table(value * factor, x_sum[f])
                head = jnp.sum(jnp.where(row_of == s, sum_top[f], 0.0), axis=0, keepdims=True)
                head = jnp.where(row_of == 0, head, result[:8])
                result = jnp.concatenate([head, result[8:]], axis=0)
                gc, gs = result[:, :LANES], result[:, LANES:]
                halves.append(
                    jnp.concatenate(
                        [gc * x_cos[...] + gs * x_sin[...], gs * x_cos[...] - gc * x_sin[...]], axis=0
                    )
                )
            result = table_times(x_first_t, jnp.concatenate(halves, axis=1))
            for e in range(2):
                send_y[f, pl.ds(2 * p + e, XA, stride=8), :] = result[:, e * LANES:(e + 1) * LANES]
            return 0

        lax.fori_loop(0, 4, sum_x, 0)
        copy = pltpu.make_async_copy(chunk(send_y.at[f], me * 8, 8), chunk(recv_y.at[f], me * 8, 8), local_sem.at[5 + f])
        copy.start()
        own.append(copy)
        send_tiles(send_y.at[f], recv_y.at[f], sends.at[2 + f], recv_sem_y.at[f])

    own_b = []
    for f in range(2):
        own[f].wait()
        remote(
            chunk(send_y.at[f], 0, most), chunk(recv_y.at[f], 0, most), sends.at[2 + f], recv_sem_y.at[f], neighbour
        ).wait_recv()

        def sum_y(g, _):
            at = pl.multiple_of(g * LANES, LANES)
            value = recv_y[f, pl.ds(at, LANES), :].T
            result = times_table(value, y_sum[f])
            bc[pl.ds(at, LANES), :] = result[:, :LANES]
            bs[pl.ds(at, LANES), :] = result[:, LANES:]

            @pl.when(g == 0)
            def _():
                result = times_table(value[:32], y_sum_top[f])
                bc[:32, :] = result[:, :LANES]
                bs[:32, :] = result[:, LANES:]

            return 0

        lax.fori_loop(0, 16, sum_y, 0)
        for q in range(4):

            def last_y(p, _):
                halves = []
                for e in range(2):
                    i = q * 8 + 2 * p + e
                    gc = bc[pl.ds(i, YA, stride=32), :]
                    gs = bs[pl.ds(i, YA, stride=32), :]
                    halves.append(
                        jnp.concatenate(
                            [gc * y_cos[...] + gs * y_sin[...], gs * y_cos[...] - gc * y_sin[...]], axis=0
                        )
                    )
                high, low = split(jnp.concatenate(halves, axis=1))
                result = dot(y_first_t[...], jnp.concatenate([high, low, high], axis=0))
                for e in range(2):
                    send_b[f, pl.ds(q * 512 + 2 * p + e, YA, stride=8), :] = result[:, e * LANES:(e + 1) * LANES]
                return 0

            lax.fori_loop(0, 4, last_y, 0)
            target = (4 * col + q) * 64
            copy = pltpu.make_async_copy(
                chunk(send_b.at[f], q * 512 + col * 64, 64), chunk(outs[f], target, 64), local_sem.at[7 + 4 * f + q]
            )
            copy.start()
            own_b.append(copy)
            for j in range(1, COLS):
                other = lax.rem(col + j, COLS)
                remote(
                    chunk(send_b.at[f], q * 512 + other * 64, 64), chunk(outs[f], target, 64),
                    sends.at[4 + f], recv_sem_b.at[f], (row, other),
                ).start()

    for copy in own_b:
        copy.wait()
    some = 4 * (COLS - 1) * 64
    for f in range(2):
        remote(chunk(send_b.at[f], 0, some), chunk(outs[f], 0, some), sends.at[4 + f], recv_sem_b.at[f], neighbour).wait()
        remote(chunk(send_y.at[f], 0, most), chunk(recv_y.at[f], 0, most), sends.at[2 + f], recv_sem_y.at[f], neighbour).wait_send()
    remote(chunk(send_x, 0, most), chunk(recv_x, 0, most), sends.at[1], recv_sem_x, neighbour).wait_send()
    remote(chunk(density, 0, some), chunk(buf, 0, some), sends.at[0], recv_sem_rows.at[0], neighbour).wait_send()


def on_device(counts, inverse_capacity):
    fixed = [jnp.asarray(table) for table in constants()]
    flat = (BINS // 4, LANES)
    vmem = pl.BlockSpec(memory_space=pltpu.VMEM)
    first, second = pl.pallas_call(
        kernel,
        out_shape=[jax.ShapeDtypeStruct(flat, F32)] * 2,
        in_specs=[vmem] * (2 + len(fixed)),
        out_specs=[vmem] * 2,
        scratch_shapes=[
            pltpu.VMEM(flat, F32),
            pltpu.VMEM(flat, F32),
            pltpu.VMEM(flat, F32),
            pltpu.VMEM(flat, F32),
            pltpu.VMEM((LANES, LANES), F32),
            pltpu.VMEM(flat, F32),
            pltpu.VMEM(flat, F32),
            pltpu.VMEM(flat, F32),
            pltpu.VMEM((8, 2 * LANES), F32),
            pltpu.VMEM((2, 8, 2 * LANES), F32),
            pltpu.VMEM((2,) + flat, F32),
            pltpu.VMEM((2,) + flat, F32),
            pltpu.VMEM((2,) + flat, F32),
            pltpu.SemaphoreType.DMA((15,)),
            pltpu.SemaphoreType.DMA((6,)),
            pltpu.SemaphoreType.DMA((4,)),
            pltpu.SemaphoreType.DMA,
            pltpu.SemaphoreType.DMA((2,)),
            pltpu.SemaphoreType.DMA((2,)),
        ],
        compiler_params=pltpu.CompilerParams(
            collective_id=0, has_side_effects=True, vmem_limit_bytes=48 * 2**20
        ),
        name="field",
    )(counts, inverse_capacity, *fixed)

    def blocked(x):
        return x.reshape(32, 8, 8, LANES).transpose(0, 2, 1, 3).reshape(256, 1024)

    return blocked(first), blocked(second)


def solution(mesh):
    return jax.shard_map(
        on_device,
        mesh=mesh,
        in_specs=(P("row", "col"), P("row", "col")),
        out_specs=(P("row", "col"), P("row", "col")),
        check_vma=False,
    )
```

time: 654 us -> 208 us (0.32)
  the two profiles are of different devices: /device:TPU:1 before, /device:TPU:31 now
where the time goes in v1:
time: 208 us; the launch traced here: 207 us
  Pallas kernels  174 us (84%)
  local copies, waits for them, and re-layouts  31.7 us (15%)
    pallas_call x1, Pallas kernels, on_device(): pl.pallas_call(kernel, out_shape=[jax.ShapeDtypeStruct(flat, F32)] * 2, i...  174 us
    unnamed x72, local copies, waits for them, and re-layouts  31.7 us

profile of v1, /device:TPU:31, one launch (start us, length us, event | category | flops | bytes accessed | tf_op | source)
XLA Modules:
  0.0 206.8 jit_solution(17161262931013060746)
XLA Ops:
  1.5 0.9 copy-done
  2.4 0.9 copy-done.1
  3.4 0.9 copy-done.2
  4.3 0.9 copy-done.3
  5.3 0.9 copy-done.4
  6.2 0.9 copy-done.5
  7.1 0.9 copy-done.6
  8.0 0.8 copy-done.8
  8.8 0.8 copy-done.9
  9.7 0.8 copy-done.10
  10.5 0.8 copy-done.11
  11.4 0.8 copy-done.12
  12.2 0.8 copy-done.13
  13.0 0.8 copy-done.14
  13.9 0.8 copy-done.15
  14.7 0.8 copy-done.16
  15.6 0.8 copy-done.17
  16.4 0.8 copy-done.18
  17.2 0.8 copy-done.19
  18.1 0.8 copy-done.20
  18.9 0.8 copy-done.21
  30.5 174.4 %field.1 = (f32[2048,128]{1,0:T(8,128)S(1)}, f32[2048,128]{1,0:T(8,128)S(1)}) custom-call(s32[256,1024]{1,0:T(8,128)} %refs_0_.1, f32[256,1024]{1,0:T(8,128)} %refs_1_.1, bf16[128,192]{1,0:T(8,128)(2,1)S(1)} %copy-done.31, bf16[64,384]{1,0:T(8,128)(2,1)S(1)} %copy-done.32, f32[64,128]{1,0:T(8,128)S(1)} %copy-done.34, f32[64,128]{1,0:T(8,128)S(1)} %copy-done.33, ...), custom_call_target="tpu_custom_call" | custom-call | tf_op jit(solution)/shard_map/field/pallas_call | solution.py:365
  204.9 1.0 copy.41
  205.8 1.0 copy.42
  (49 shorter events, 11.6 us)
Async XLA Ops:
  0.6 0.8 copy-start.7
  1.5 0.9 copy-start
  2.4 0.9 copy-start.1
  3.4 0.9 copy-start.2
  4.3 0.9 copy-start.3
  5.3 0.9 copy-start.4
  6.2 0.9 copy-start.5
  7.1 0.9 copy-start.6
  8.0 0.8 copy-start.8
  8.8 0.8 copy-start.9
  9.7 0.8 copy-start.10
  10.5 0.8 copy-start.11
  11.3 0.8 copy-start.12
  12.2 0.8 copy-start.13
  13.0 0.8 copy-start.14
  13.9 0.8 copy-start.15
  14.7 0.8 copy-start.16
  15.5 0.8 copy-start.17
  16.4 0.8 copy-start.18
  17.2 0.8 copy-start.19
  18.1 0.8 copy-start.20
  18.9 0.8 copy-start.21
  19.7 0.8 copy-start.22
  20.6 0.8 copy-start.23
  (11 other events, 9.0 us)

commit v2 on v1

v2 whole, which is shorter than its diff:
```python
import math

import jax
import jax.numpy as jnp
import numpy as np
from jax import lax
from jax.experimental import pallas as pl
from jax.experimental.pallas import tpu as pltpu
from jax.sharding import PartitionSpec as P

MESH = pl.DeviceIdType.MESH
F32 = jnp.float32
BF16 = jnp.bfloat16
ROWS, COLS = 32, 8
DEVICES = ROWS * COLS
LANES = 128
YA, YB = 64, 128
XA, XB = 256, 32
BINS = 8192


def tables(coarse, fine):
    half = fine // 2
    k = np.arange(coarse)[:, None]
    a = np.arange(coarse)[None, :]
    angle = np.pi * (k * a % (2 * coarse)) / coarse
    first = np.concatenate([np.cos(angle), np.sin(angle)], axis=0)
    first[coarse] = 1.0 - 2.0 * (np.arange(coarse) % 2)
    odd = 2 * np.arange(fine)[None, :] + 1
    turn = np.pi * k * odd / (2 * coarse * fine)
    m = np.arange(half)[:, None]
    low = np.pi * (m * odd % (2 * fine)) / fine
    high = np.pi * ((m + 1) * odd % (2 * fine)) / fine
    middle = np.pi * ((2 * m + 1) * odd % (4 * fine)) / (2 * fine)
    zero = np.zeros_like(low)
    cosine = np.block([[np.cos(low), -np.sin(low)], [np.cos(high), np.sin(high)]])
    cosine_top = np.block([[np.cos(low), zero], [zero, np.cos(middle)]])
    sine = np.block([[np.sin(low), np.cos(low)], [np.sin(high), -np.cos(high)]])
    sine_top = np.block([[np.sin(low), zero], [zero, np.sin(middle)]])
    place = np.arange(fine)[None, :]
    index = np.where(place < half, k + 2 * coarse * place, 2 * coarse * (place - half + 1) - k)
    index[0] = np.where(place[0] < half, 2 * coarse * place[0], coarse + 2 * coarse * (place[0] - half))
    return first, turn, cosine, cosine_top, sine, sine_top, index


def spread(matrix, copies):
    size = matrix.shape[0]
    left = np.kron(np.eye(copies), matrix[:, :size])
    right = np.kron(np.eye(copies), matrix[:, size:])
    return np.concatenate([left, right], axis=1)


def constants():
    products, singles = [], []
    first, turn, cosine, cosine_top, sine, sine_top, _ = tables(YA, YB)
    products += [("y_first", np.concatenate([first, np.zeros_like(first)], axis=1)), ("y_first_t", first.T)]
    singles += [("y_cos", np.cos(turn)), ("y_sin", np.sin(turn))]

    def seconds(axis, cosine, cosine_top, sine, sine_top):
        found = [(axis + "_second", cosine.T), (axis + "_second_top", cosine_top.T)]
        for name, table in (("_cos", cosine), ("_cos_top", cosine_top), ("_sin", sine), ("_sin_top", sine_top)):
            found += [(axis + name, table)]
        return found

    products += seconds("y", cosine, cosine_top, sine, sine_top)
    first, turn, cosine, cosine_top, sine, sine_top, index = tables(XA, XB)
    copies = LANES // XB
    products += [("x_first", first), ("x_first_t", first.T)]
    singles += [(name, np.tile(t, (1, copies))) for name, t in
                (("x_cos", np.cos(turn)), ("x_sin", np.sin(turn)), ("x_index", index))]
    products += seconds("x", *(spread(t, copies) for t in (cosine, cosine_top, sine, sine_top)))

    def pack(named):
        at, places = 0, {}
        for name, table in named:
            places[name] = (at, table.shape)
            at += table.size // LANES
        tiled = [
            table[:, lane:lane + LANES] for _, table in named for lane in range(0, table.shape[1], LANES)
        ]
        return np.concatenate(tiled, axis=0).astype(np.float32), places

    return pack(products) + pack(singles)


PRODUCTS, PRODUCT_AT, SINGLES, SINGLE_AT = constants()


def split(x):
    high = x.astype(BF16)
    return high, (x - high.astype(F32)).astype(BF16)


def dot(x, y):
    return jnp.dot(x, y, preferred_element_type=F32)


def times_table(x, table):
    high, low = split(x)
    t_high, t_low = table()
    return dot(high, t_high) + dot(low, t_high) + dot(high, t_low)


def table_times(table, x):
    high, low = split(x)
    t_high, t_low = table()
    return dot(t_high, high) + dot(t_high, low) + dot(t_low, high)


def kernel(
    counts_hbm, inverse_hbm, products_hbm, singles_hbm, out_first, out_second,
    counts, inverse, products, singles, table_high, table_low, y_stack, density, buf, bc, bs, turned, send_x, recv_x, spec, spec_top, sum_top,
    send_y, recv_y, send_b, load_sem, local_sem, sends, recv_sem_rows, recv_sem_x, recv_sem_y, recv_sem_b,
):
    def single(name):
        at, (height, _) = SINGLE_AT[name]
        return singles[at:at + height, :]

    def table(name):
        at, (height, width) = PRODUCT_AT[name]
        return lambda: [
            jnp.concatenate([part[at + t * height:at + (t + 1) * height, :] for t in range(width // LANES)], axis=1)
            for part in (table_high, table_low)
        ]

    outs = [out_first, out_second]
    pending = []
    loads = [
        pltpu.make_async_copy(counts_hbm, counts, load_sem.at[0]),
        pltpu.make_async_copy(inverse_hbm, inverse, load_sem.at[1]),
        pltpu.make_async_copy(products_hbm, products, load_sem.at[2]),
        pltpu.make_async_copy(singles_hbm, singles, load_sem.at[3]),
    ]
    for copy in loads:
        copy.start()

    row = lax.axis_index("row")
    col = lax.axis_index("col")
    me = row * COLS + col

    def place(device):
        return (device // COLS, device % COLS)

    def remote(src, dst, send, recv, device):
        return pltpu.make_async_remote_copy(
            src_ref=src, dst_ref=dst, send_sem=send, recv_sem=recv, device_id=device, device_id_type=MESH
        )

    barrier = pltpu.get_barrier_semaphore()

    for j in range(1, COLS):
        pl.semaphore_signal(barrier, inc=1, device_id=(row, lax.rem(col + j, COLS)), device_id_type=MESH)

    def greet(j, _):
        pl.semaphore_signal(barrier, inc=1, device_id=(lax.rem(row + j, ROWS), col), device_id_type=MESH)
        return 0

    lax.fori_loop(1, ROWS, greet, 0)

    loads[0].wait()
    loads[1].wait()

    def make_density(t, _):
        owner, q = t // 4, t % 4
        at = pl.multiple_of(t * 8, 8)
        values = counts[pl.ds(at, 8), :].astype(F32) * inverse[pl.ds(at, 8), :] * 0.03125
        for tile in range(8):
            density[pl.ds(pl.multiple_of(t * 64 + tile * 8, 8), 8), :] = values[:, tile * LANES:(tile + 1) * LANES]
        return 0

    lax.fori_loop(0, 32, make_density, 0)
    pl.semaphore_wait(barrier, ROWS + COLS - 2)

    def chunk(ref, at, size):
        return ref.at[pl.ds(pl.multiple_of(at, 8), size), :]

    own = []
    for q in range(4):
        copy = pltpu.make_async_copy(chunk(density, col * 256 + q * 64, 64), chunk(buf, q * 512 + col * 64, 64), local_sem.at[q])
        copy.start()
        own.append(copy)
        for j in range(1, COLS):
            other = lax.rem(col + j, COLS)
            remote(
                chunk(density, other * 256 + q * 64, 64), chunk(buf, q * 512 + col * 64, 64),
                sends.at[0], recv_sem_rows.at[q], (row, other),
            ).start()

    neighbour = (row, lax.rem(col + 1, COLS))

    loads[2].wait()
    loads[3].wait()

    def split_tables(t, _):
        at = pl.ds(pl.multiple_of(t * 64, 64), 64)
        table_high[at, :], table_low[at, :] = split(products[at, :])
        return 0

    lax.fori_loop(0, PRODUCTS.shape[0] // 64, split_tables, 0)
    high, low = (part[:, :YA] for part in table("y_first")())
    y_stack[...] = jnp.concatenate([high, high, low], axis=1)
    for q in range(4):
        own[q].wait()
        whole = chunk(buf, 0, (COLS - 1) * 64)
        remote(whole, whole, sends.at[0], recv_sem_rows.at[q], neighbour).wait_recv()

        def first_y(p, _):
            at = q * 512 + 2 * p
            pair = jnp.concatenate(
                [buf[pl.ds(at, YA, stride=8), :], buf[pl.ds(at + 1, YA, stride=8), :]], axis=1
            )
            high, low = split(pair)
            result = dot(y_stack[...], jnp.concatenate([high, low, high], axis=0))
            for e in range(2):
                i = q * 8 + 2 * p + e
                ac = result[:YA, e * LANES:(e + 1) * LANES]
                as_ = result[YA:, e * LANES:(e + 1) * LANES]
                bc[pl.ds(i, YA, stride=32), :] = ac * single("y_cos") - as_ * single("y_sin")
                bs[pl.ds(i, YA, stride=32), :] = ac * single("y_sin") + as_ * single("y_cos")
            return 0

        lax.fori_loop(0, 4, first_y, 0)

    def second_y(t, _):
        at = pl.multiple_of(t * 512, 512)
        both = jnp.concatenate([bc[pl.ds(at, 512), :], bs[pl.ds(at, 512), :]], axis=1)
        turned[...] = times_table(both, table("y_second"))

        @pl.when(t == 0)
        def _():
            turned[:32, :] = times_table(both[:32], table("y_second_top"))

        for g in range(4):
            block = turned[g * LANES:(g + 1) * LANES, :].T
            for h in range(2):
                send_x.at[h].reshape(1024, LANES)[pl.ds(pl.multiple_of(t * 256 + g * 64, 64), 64), :] = block[h * 64:(h + 1) * 64]
        return 0

    lax.fori_loop(0, 4, second_y, 0)

    def exchange(src, dst, send, recv, local):
        copy = pltpu.make_async_copy(src.at[me], dst.at[me], local)
        copy.start()

        def step(j, _):
            for e in range(5):
                other = lax.rem(me + 1 + 5 * j + e, DEVICES)
                remote(src.at[other], dst.at[me], send, recv, place(other)).start()
            return 0

        lax.fori_loop(0, (DEVICES - 1) // 5, step, 0)
        rest = remote(src.at[pl.ds(0, DEVICES - 1)], dst.at[pl.ds(0, DEVICES - 1)], send, recv, neighbour)
        pending.append(rest.wait_send)

        def arrived():
            copy.wait()
            rest.wait_recv()

        return arrived

    arrived_x = [
        exchange(send_x.at[h], recv_x.at[h], sends.at[1 + h], recv_sem_x.at[h], local_sem.at[4 + h]) for h in range(2)
    ]
    spec_top[...] = jnp.zeros_like(spec_top)
    row_of = lax.broadcasted_iota(jnp.int32, (8, 2 * LANES), 0)
    norming = 4.0 / math.sqrt(BINS * BINS) / math.pi

    def v_of(half, step, shape):
        k = 4 * (me // 16) + lax.broadcasted_iota(jnp.int32, shape, 1) // XB
        m = 4 * lax.rem(me, 16) + step
        if half == 0:
            return (k + 2 * YA * m).astype(F32)
        return jnp.where(k == 0, 2 * YA * m + YA, 2 * YA * (m + 1) - k).astype(F32)

    arrived_y = {}
    for h in range(2):
        arrived_x[h]()
        pieces = recv_x.at[h].reshape(1024, LANES)

        def first_x(p, _):
            pair = jnp.concatenate(
                [pieces[pl.ds(2 * p, XA, stride=4), :], pieces[pl.ds(2 * p + 1, XA, stride=4), :]], axis=1
            )
            result = table_times(table("x_first"), pair)
            for e in range(2):
                s = 2 * p + e
                ac = result[:XA, e * LANES:(e + 1) * LANES]
                as_ = result[XA:, e * LANES:(e + 1) * LANES]
                both = jnp.concatenate(
                    [ac * single("x_cos") - as_ * single("x_sin"), ac * single("x_sin") + as_ * single("x_cos")],
                    axis=1,
                )
                spec[pl.ds(pl.multiple_of(s * XA, XA), XA), :] = times_table(both, table("x_second"))
                spec_top[pl.ds(s, 1), :] = both[:1]
            return 0

        lax.fori_loop(0, 2, first_x, 0)
        spec[pl.ds(0, 4, stride=XA), :] = times_table(spec_top[...], table("x_second_top"))[:4]

        def weigh(s, _):
            at = pl.multiple_of(s * XA, XA)
            v_row = v_of(h, s, (1, LANES))
            u = single("x_index")
            square = u * u + v_row * v_row
            corner = square == 0.0
            weight = jnp.where(corner, 0.0, norming / jnp.where(corner, 1.0, square))
            spec[pl.ds(at, XA), :] = spec[pl.ds(at, XA), :] * weight
            return 0

        lax.fori_loop(0, 4, weigh, 0)
        top = spec[pl.ds(0, 4, stride=XA), :]
        top = jnp.concatenate([top, jnp.zeros_like(top)], axis=0)
        tops = [
            times_table(top * single("x_index")[:1], table("x_sin_top")),
            times_table(top * v_of(h, lax.broadcasted_iota(jnp.int32, (8, LANES), 0), (8, LANES)), table("x_cos_top")),
        ]
        for f in range(2):
            sum_top[f] = tops[f]

        for f in range(2):
            target = send_y.at[f, h].reshape(1024, LANES)

            def sum_x(p, _):
                both = []
                for e in range(2):
                    s = 2 * p + e
                    value = spec[pl.ds(pl.multiple_of(s * XA, XA), XA), :]
                    factor = single("x_index") if f == 0 else v_of(h, s, (1, LANES))
                    result = times_table(value * factor, table(("x_sin", "x_cos")[f]))
                    head = jnp.sum(jnp.where(row_of == s, sum_top[f], 0.0), axis=0, keepdims=True)
                    head = jnp.where(row_of == 0, head, result[:8])
                    result = jnp.concatenate([head, result[8:]], axis=0)
                    gc, gs = result[:, :LANES], result[:, LANES:]
                    both.append(
                        jnp.concatenate(
                            [gc * single("x_cos") + gs * single("x_sin"), gs * single("x_cos") - gc * single("x_sin")],
                            axis=0,
                        )
                    )
                result = table_times(table("x_first_t"), jnp.concatenate(both, axis=1))
                for e in range(2):
                    target[pl.ds(2 * p + e, XA, stride=4), :] = result[:, e * LANES:(e + 1) * LANES]
                return 0

            lax.fori_loop(0, 2, sum_x, 0)
            arrived_y[f, h] = exchange(
                send_y.at[f, h], recv_y.at[f, h], sends.at[3 + 2 * f + h], recv_sem_y.at[2 * f + h],
                local_sem.at[6 + 2 * f + h],
            )

    for f in range(2):
        for h in range(2):
            arrived_y[f, h]()

        def sum_y(g, _):
            at = pl.multiple_of(g * LANES, LANES)
            half = pl.ds(pl.multiple_of(g * 64, 64), 64)
            value = jnp.concatenate([recv_y.at[f, h].reshape(1024, LANES)[half, :] for h in range(2)], axis=0).T
            result = times_table(value, table(("y_cos", "y_sin")[f]))
            bc[pl.ds(at, LANES), :] = result[:, :LANES]
            bs[pl.ds(at, LANES), :] = result[:, LANES:]

            @pl.when(g == 0)
            def _():
                result = times_table(value[:32], table(("y_cos_top", "y_sin_top")[f]))
                bc[:32, :] = result[:, :LANES]
                bs[:32, :] = result[:, LANES:]

            return 0

        lax.fori_loop(0, 16, sum_y, 0)
        for q in range(4):

            def last_y(p, _):
                both = []
                for e in range(2):
                    i = q * 8 + 2 * p + e
                    gc = bc[pl.ds(i, YA, stride=32), :]
                    gs = bs[pl.ds(i, YA, stride=32), :]
                    both.append(
                        jnp.concatenate(
                            [gc * single("y_cos") + gs * single("y_sin"), gs * single("y_cos") - gc * single("y_sin")], axis=0
                        )
                    )
                result = table_times(table("y_first_t"), jnp.concatenate(both, axis=1))
                for e in range(2):
                    send_b[f, pl.ds(q * 512 + 2 * p + e, YA, stride=8), :] = result[:, e * LANES:(e + 1) * LANES]
                return 0

            lax.fori_loop(0, 4, last_y, 0)
            target = (4 * col + q) * 64
            copy = pltpu.make_async_copy(
                chunk(send_b.at[f], q * 512 + col * 64, 64), chunk(outs[f], target, 64), local_sem.at[10 + 4 * f + q]
            )
            copy.start()
            pending.append(copy.wait)
            for j in range(1, COLS):
                other = lax.rem(col + j, COLS)
                remote(
                    chunk(send_b.at[f], q * 512 + other * 64, 64), chunk(outs[f], target, 64),
                    sends.at[7 + f], recv_sem_b.at[f], (row, other),
                ).start()

    some = 4 * (COLS - 1) * 64
    for f in range(2):
        remote(chunk(send_b.at[f], 0, some), chunk(outs[f], 0, some), sends.at[7 + f], recv_sem_b.at[f], neighbour).wait()
    remote(chunk(density, 0, some), chunk(buf, 0, some), sends.at[0], recv_sem_rows.at[0], neighbour).wait_send()
    for wait in pending:
        wait()


def on_device(counts, inverse_capacity):
    flat = (BINS // 4, LANES)
    vmem = pl.BlockSpec(memory_space=pltpu.VMEM)
    hbm = pl.BlockSpec(memory_space=pltpu.HBM)
    first, second = pl.pallas_call(
        kernel,
        out_shape=[jax.ShapeDtypeStruct(flat, F32)] * 2,
        in_specs=[hbm] * 4,
        out_specs=[vmem] * 2,
        scratch_shapes=[
            pltpu.VMEM(counts.shape, jnp.int32),
            pltpu.VMEM(counts.shape, F32),
            pltpu.VMEM(PRODUCTS.shape, F32),
            pltpu.VMEM(SINGLES.shape, F32),
            pltpu.VMEM(PRODUCTS.shape, BF16),
            pltpu.VMEM(PRODUCTS.shape, BF16),
            pltpu.VMEM((2 * YA, 3 * YA), BF16),
            pltpu.VMEM(flat, F32),
            pltpu.VMEM(flat, F32),
            pltpu.VMEM(flat, F32),
            pltpu.VMEM(flat, F32),
            pltpu.VMEM((4 * LANES, LANES), F32),
            pltpu.VMEM((2, DEVICES, 4, LANES), F32),
            pltpu.VMEM((2, DEVICES, 4, LANES), F32),
            pltpu.VMEM((1024, LANES), F32),
            pltpu.VMEM((8, 2 * LANES), F32),
            pltpu.VMEM((2, 8, 2 * LANES), F32),
            pltpu.VMEM((2, 2, DEVICES, 4, LANES), F32),
            pltpu.VMEM((2, 2, DEVICES, 4, LANES), F32),
            pltpu.VMEM((2,) + flat, F32),
            pltpu.SemaphoreType.DMA((4,)),
            pltpu.SemaphoreType.DMA((18,)),
            pltpu.SemaphoreType.DMA((9,)),
            pltpu.SemaphoreType.DMA((4,)),
            pltpu.SemaphoreType.DMA((2,)),
            pltpu.SemaphoreType.DMA((4,)),
            pltpu.SemaphoreType.DMA((2,)),
        ],
        compiler_params=pltpu.CompilerParams(
            collective_id=0, has_side_effects=True, vmem_limit_bytes=58 * 2**20
        ),
        name="field",
    )(counts, inverse_capacity, jnp.asarray(PRODUCTS), jnp.asarray(SINGLES))

    def blocked(x):
        return x.reshape(32, 8, 8, LANES).transpose(0, 2, 1, 3).reshape(256, 1024)

    return blocked(first), blocked(second)


def solution(mesh):
    return jax.shard_map(
        on_device,
        mesh=mesh,
        in_specs=(P("row", "col"), P("row", "col")),
        out_specs=(P("row", "col"), P("row", "col")),
        check_vma=False,
    )
```

time: 208 us -> 159 us (0.76)
  the two profiles are of different devices: /device:TPU:31 before, /device:TPU:1 now
where the time goes in v2:
time: 159 us
  Pallas kernels  155 us (97%)
  local copies, waits for them, and re-layouts  3.37 us (2%)
    pallas_call x1, Pallas kernels, on_device(): pl.pallas_call(kernel, out_shape=[jax.ShapeDtypeStruct(flat, F32)] * 2, i...  155 us
    unnamed x4, local copies, waits for them, and re-layouts  3.37 us

profile of v2, /device:TPU:1, one launch (start us, length us, event | category | flops | bytes accessed | tf_op | source)
XLA Modules:
  0.0 159.2 jit_solution(11003807748993309230)
XLA Ops:
  0.6 155.2 %field.1 = (f32[2048,128]{1,0:T(8,128)}, f32[2048,128]{1,0:T(8,128)}) custom-call(s32[256,1024]{1,0:T(8,128)} %counts_hbm.1, f32[256,1024]{1,0:T(8,128)} %inverse_hbm.1, f32[5312,128]{1,0:T(8,128)} %constant.4.clone.products_hbm, f32[896,128]{1,0:T(8,128)} %constant.5.clone.singles_hbm), custom_call_target="tpu_custom_call" | custom-call | tf_op jit(solution)/shard_map/field/pallas_call | solution.py:416
  155.8 0.0 copy-start
  155.9 2.4 %copy.8 = f32[256,1024]{1,0:T(8,128)} copy(f32[256,1024]{1,0:T(8,128)} %bitcast.11) | data formatting | bytes 2097152
  158.3 0.0 copy-done
  158.3 1.0 copy.9
Async XLA Ops:
  155.8 2.4 %copy-start = (f32[2048,128]{1,0:T(8,128)S(1)}, f32[2048,128]{1,0:T(8,128)}, u32[]{:S(2)}) copy-start(f32[2048,128]{1,0:T(8,128)} %get-tuple-element.5) | copy-start | bytes 3145732

commit v3 on v2

--- a/solution.py
+++ b/solution.py
@@ -160,23 +160,27 @@
     loads[0].wait()
     loads[1].wait()
 
-    def make_density(t, _):
-        owner, q = t // 4, t % 4
-        at = pl.multiple_of(t * 8, 8)
-        values = counts[pl.ds(at, 8), :].astype(F32) * inverse[pl.ds(at, 8), :] * 0.03125
-        for tile in range(8):
-            density[pl.ds(pl.multiple_of(t * 64 + tile * 8, 8), 8), :] = values[:, tile * LANES:(tile + 1) * LANES]
-        return 0
-
-    lax.fori_loop(0, 32, make_density, 0)
-    pl.semaphore_wait(barrier, ROWS + COLS - 2)
-
     def chunk(ref, at, size):
         return ref.at[pl.ds(pl.multiple_of(at, 8), size), :]
 
     own = []
     for q in range(4):
-        copy = pltpu.make_async_copy(chunk(density, col * 256 + q * 64, 64), chunk(buf, q * 512 + col * 64, 64), local_sem.at[q])
+
+        def make_density(owner, _):
+            at = pl.multiple_of(owner * 32 + q * 8, 8)
+            values = counts[pl.ds(at, 8), :].astype(F32) * inverse[pl.ds(at, 8), :] * 0.03125
+            for tile in range(8):
+                to = pl.multiple_of(owner * 256 + q * 64 + tile * 8, 8)
+                density[pl.ds(to, 8), :] = values[:, tile * LANES:(tile + 1) * LANES]
+            return 0
+
+        lax.fori_loop(0, 8, make_density, 0)
+        if q == 0:
+            pl.semaphore_wait(barrier, ROWS + COLS - 2)
+
+        copy = pltpu.make_async_copy(
+            chunk(density, col * 256 + q * 64, 64), chunk(buf, q * 512 + col * 64, 64), local_sem.at[q]
+        )
         copy.start()
         own.append(copy)
         for j in range(1, COLS):
@@ -221,46 +225,65 @@
 
         lax.fori_loop(0, 4, first_y, 0)
 
+    def send_piece(src, dst, send, recv, other):
+        remote(src.at[other], dst.at[me], send, recv, place(other)).start()
+
+    def settle(src, dst, send, recv, local):
+        copy = pltpu.make_async_copy(src.at[me], dst.at[me], local)
+        copy.start()
+        rest = remote(src.at[pl.ds(0, DEVICES - 1)], dst.at[pl.ds(0, DEVICES - 1)], send, recv, neighbour)
+        pending.append(rest.wait_send)
+
+        def arrived():
+            copy.wait()
+            rest.wait_recv()
+
+        return arrived
+
+    def exchange(src, dst, send, recv, local):
+        def step(j, _):
+            for e in range(5):
+                send_piece(src, dst, send, recv, lax.rem(me + 1 + 5 * j + e, DEVICES))
+            return 0
+
+        lax.fori_loop(0, (DEVICES - 1) // 5, step, 0)
+        return settle(src, dst, send, recv, local)
+
+    channel = [
+        (send_x.at[h], recv_x.at[h], sends.at[1 + h], recv_sem_x.at[h], local_sem.at[4 + h]) for h in range(2)
+    ]
+
     def second_y(t, _):
-        at = pl.multiple_of(t * 512, 512)
+        first = lax.rem(me // 64 + t, 4)
+        at = pl.multiple_of(first * 512, 512)
         both = jnp.concatenate([bc[pl.ds(at, 512), :], bs[pl.ds(at, 512), :]], axis=1)
         turned[...] = times_table(both, table("y_second"))
 
-        @pl.when(t == 0)
+        @pl.when(first == 0)
         def _():
             turned[:32, :] = times_table(both[:32], table("y_second_top"))
 
         for g in range(4):
             block = turned[g * LANES:(g + 1) * LANES, :].T
             for h in range(2):
-                send_x.at[h].reshape(1024, LANES)[pl.ds(pl.multiple_of(t * 256 + g * 64, 64), 64), :] = block[h * 64:(h + 1) * 64]
+                to = pl.multiple_of(first * 256 + g * 64, 64)
+                send_x.at[h].reshape(1024, LANES)[pl.ds(to, 64), :] = block[h * 64:(h + 1) * 64]
+
+        def step(other, _):
+            send_piece(*channel[0][:4], other)
+            return 0
+
+        lax.fori_loop(jnp.where(t == 0, me + 1, first * 64), first * 64 + 64, step, 0)
         return 0
 
     lax.fori_loop(0, 4, second_y, 0)
 
-    def exchange(src, dst, send, recv, local):
-        copy = pltpu.make_async_copy(src.at[me], dst.at[me], local)
-        copy.start()
-
-        def step(j, _):
-            for e in range(5):
-                other = lax.rem(me + 1 + 5 * j + e, DEVICES)
-                remote(src.at[other], dst.at[me], send, recv, place(other)).start()
-            return 0
-
-        lax.fori_loop(0, (DEVICES - 1) // 5, step, 0)
-        rest = remote(src.at[pl.ds(0, DEVICES - 1)], dst.at[pl.ds(0, DEVICES - 1)], send, recv, neighbour)
-        pending.append(rest.wait_send)
-
-        def arrived():
-            copy.wait()
-            rest.wait_recv()
-
-        return arrived
-
-    arrived_x = [
-        exchange(send_x.at[h], recv_x.at[h], sends.at[1 + h], recv_sem_x.at[h], local_sem.at[4 + h]) for h in range(2)
-    ]
+    def rest_of_own(other, _):
+        send_piece(*channel[0][:4], other)
+        return 0
+
+    lax.fori_loop(me // 64 * 64, me, rest_of_own, 0)
+    arrived_x = [settle(*channel[0]), exchange(*channel[1])]
     spec_top[...] = jnp.zeros_like(spec_top)
     row_of = lax.broadcasted_iota(jnp.int32, (8, 2 * LANES), 0)
     norming = 4.0 / math.sqrt(BINS * BINS) / math.pi
@@ -448,10 +471,13 @@
             pltpu.SemaphoreType.DMA((2,)),
         ],
         compiler_params=pltpu.CompilerParams(
-            collective_id=0, has_side_effects=True, vmem_limit_bytes=58 * 2**20
+            collective_id=0, has_side_effects=True, vmem_limit_bytes=48 * 2**20
         ),
         name="field",
-    )(counts, inverse_capacity, jnp.asarray(PRODUCTS), jnp.asarray(SINGLES))
+    )(*[
+        pltpu.with_memory_space_constraint(x, pltpu.HBM)
+        for x in (counts, inverse_capacity, jnp.asarray(PRODUCTS), jnp.asarray(SINGLES))
+    ])
 
     def blocked(x):
         return x.reshape(32, 8, 8, LANES).transpose(0, 2, 1, 3).reshape(256, 1024)

time: 159 us -> 155 us (0.975)
  Pallas kernels: 155 us -> 152 us
    pallas_call x1, Pallas kernels: 155 us -> 152 us  [on_device(): pl.pallas_call(kernel, out_shape=[jax.ShapeDtypeStruct(flat, F32)] * 2, i...]
    unnamed x4 -> x2, local copies, waits for them, and re-layouts: 3.37 us -> 1.94 us
where the time goes in v3:
time: 155 us
  Pallas kernels  152 us (98%)
  local copies, waits for them, and re-layouts  1.94 us (1%)
    pallas_call x1, Pallas kernels, on_device(): pl.pallas_call(kernel, out_shape=[jax.ShapeDtypeStruct(flat, F32)] * 2, i...  152 us

profile of v3, /device:TPU:1, one launch (start us, length us, event | category | flops | bytes accessed | tf_op | source)
XLA Modules:
  0.0 155.0 jit_solution(13142821276418343822)
XLA Ops:
  0.6 152.4 %field.1 = (f32[2048,128]{1,0:T(8,128)S(1)}, f32[2048,128]{1,0:T(8,128)S(1)}) custom-call(s32[256,1024]{1,0:T(8,128)} %counts_hbm.1, f32[256,1024]{1,0:T(8,128)} %inverse_hbm.1, f32[5312,128]{1,0:T(8,128)} %constant.4.clone.products_hbm, f32[896,128]{1,0:T(8,128)} %constant.5.clone.singles_hbm), custom_call_target="tpu_custom_call" | custom-call | tf_op jit(solution)/shard_map/field/pallas_call | solution.py:439
  153.0 1.0 copy.8
  154.0 1.0 copy.9

commit v4 on v3

--- a/solution.py
+++ b/solution.py
@@ -223,7 +223,7 @@
                 bs[pl.ds(i, YA, stride=32), :] = ac * single("y_sin") + as_ * single("y_cos")
             return 0
 
-        lax.fori_loop(0, 4, first_y, 0)
+        lax.fori_loop(0, 4, first_y, 0, unroll=True)
 
     def send_piece(src, dst, send, recv, other):
         remote(src.at[other], dst.at[me], send, recv, place(other)).start()
@@ -317,7 +317,7 @@
                 spec_top[pl.ds(s, 1), :] = both[:1]
             return 0
 
-        lax.fori_loop(0, 2, first_x, 0)
+        lax.fori_loop(0, 2, first_x, 0, unroll=True)
         spec[pl.ds(0, 4, stride=XA), :] = times_table(spec_top[...], table("x_second_top"))[:4]
 
         def weigh(s, _):
@@ -330,7 +330,7 @@
             spec[pl.ds(at, XA), :] = spec[pl.ds(at, XA), :] * weight
             return 0
 
-        lax.fori_loop(0, 4, weigh, 0)
+        lax.fori_loop(0, 4, weigh, 0, unroll=True)
         top = spec[pl.ds(0, 4, stride=XA), :]
         top = jnp.concatenate([top, jnp.zeros_like(top)], axis=0)
         tops = [
@@ -365,7 +365,7 @@
                     target[pl.ds(2 * p + e, XA, stride=4), :] = result[:, e * LANES:(e + 1) * LANES]
                 return 0
 
-            lax.fori_loop(0, 2, sum_x, 0)
+            lax.fori_loop(0, 2, sum_x, 0, unroll=True)
             arrived_y[f, h] = exchange(
                 send_y.at[f, h], recv_y.at[f, h], sends.at[3 + 2 * f + h], recv_sem_y.at[2 * f + h],
                 local_sem.at[6 + 2 * f + h],
@@ -410,7 +410,7 @@
                     send_b[f, pl.ds(q * 512 + 2 * p + e, YA, stride=8), :] = result[:, e * LANES:(e + 1) * LANES]
                 return 0
 
-            lax.fori_loop(0, 4, last_y, 0)
+            lax.fori_loop(0, 4, last_y, 0, unroll=True)
             target = (4 * col + q) * 64
             copy = pltpu.make_async_copy(
                 chunk(send_b.at[f], q * 512 + col * 64, 64), chunk(outs[f], target, 64), local_sem.at[10 + 4 * f + q]
@@ -430,6 +430,14 @@
     remote(chunk(density, 0, some), chunk(buf, 0, some), sends.at[0], recv_sem_rows.at[0], neighbour).wait_send()
     for wait in pending:
         wait()
+
+
+def settle_kernel(a, b, to_a, to_b, sem):
+    copies = [pltpu.make_async_copy(a, to_a, sem.at[0]), pltpu.make_async_copy(b, to_b, sem.at[1])]
+    for copy in copies:
+        copy.start()
+    for copy in copies:
+        copy.wait()
 
 
 def on_device(counts, inverse_capacity):
@@ -479,6 +487,16 @@
         for x in (counts, inverse_capacity, jnp.asarray(PRODUCTS), jnp.asarray(SINGLES))
     ])
 
+    first, second = pl.pallas_call(
+        settle_kernel,
+        out_shape=[jax.ShapeDtypeStruct(flat, F32)] * 2,
+        in_specs=[pl.BlockSpec(memory_space=pl.ANY)] * 2,
+        out_specs=[hbm] * 2,
+        scratch_shapes=[pltpu.SemaphoreType.DMA((2,))],
+        compiler_params=pltpu.CompilerParams(vmem_limit_bytes=2**20),
+        name="settle",
+    )(first, second)
+
     def blocked(x):
         return x.reshape(32, 8, 8, LANES).transpose(0, 2, 1, 3).reshape(256, 1024)
 

time: 155 us -> 154 us (level)
  Pallas kernels: 152 us -> 154 us
  local copies, waits for them, and re-layouts: 1.94 us -> 0 us
    unnamed x2 -> x0, local copies, waits for them, and re-layouts: 1.94 us -> none
where the time goes in v4:
time: 154 us
  Pallas kernels  154 us (100%)
    pallas_call x1, Pallas kernels, on_device(): pl.pallas_call(kernel, out_shape=[jax.ShapeDtypeStruct(flat, F32)] * 2, i...  152 us

profile of v4, /device:TPU:1, one launch (start us, length us, event | category | flops | bytes accessed | tf_op | source)
XLA Modules:
  0.0 154.3 jit_solution(12864093591816779284)
XLA Ops:
  0.6 152.2 %field.1 = (f32[2048,128]{1,0:T(8,128)S(1)}, f32[2048,128]{1,0:T(8,128)S(1)}) custom-call(s32[256,1024]{1,0:T(8,128)} %counts_hbm.1, f32[256,1024]{1,0:T(8,128)} %inverse_hbm.1, f32[5312,128]{1,0:T(8,128)} %constant.4.clone.products_hbm, f32[896,128]{1,0:T(8,128)} %constant.5.clone.singles_hbm), custom_call_target="tpu_custom_call" | custom-call | tf_op jit(solution)/shard_map/field/pallas_call | solution.py:447
  152.8 1.3 settle.1

commit v5 on v4

--- a/solution.py
+++ b/solution.py
@@ -50,6 +50,14 @@
     return np.concatenate([left, right], axis=1)
 
 
+def paired(table, field):
+    out = np.zeros_like(table)
+    for group in range(YB // 8):
+        at = 8 * group + 4 * field
+        out[at:at + 4] = table[4 * group:4 * group + 4]
+    return out
+
+
 def constants():
     products, singles = [], []
     first, turn, cosine, cosine_top, sine, sine_top, _ = tables(YA, YB)
@@ -59,7 +67,10 @@
     def seconds(axis, cosine, cosine_top, sine, sine_top):
         found = [(axis + "_second", cosine.T), (axis + "_second_top", cosine_top.T)]
         for name, table in (("_cos", cosine), ("_cos_top", cosine_top), ("_sin", sine), ("_sin_top", sine_top)):
-            found += [(axis + name, table)]
+            if axis == "x":
+                found += [(axis + name, table)]
+            else:
+                found += [(axis + name, paired(table, int("sin" in name))), (axis + name + "_rest", table[YB // 2:])]
         return found
 
     products += seconds("y", cosine, cosine_top, sine, sine_top)
@@ -110,7 +121,7 @@
 def kernel(
     counts_hbm, inverse_hbm, products_hbm, singles_hbm, out_first, out_second,
     counts, inverse, products, singles, table_high, table_low, y_stack, density, buf, bc, bs, turned, send_x, recv_x, spec, spec_top, sum_top,
-    send_y, recv_y, send_b, load_sem, local_sem, sends, recv_sem_rows, recv_sem_x, recv_sem_y, recv_sem_b,
+    send_pair, recv_pair, send_y, recv_y, send_b, load_sem, local_sem, sends, recv_sem_rows, recv_sem_x, recv_sem_y, recv_sem_b,
 ):
     def single(name):
         at, (height, _) = SINGLE_AT[name]
@@ -341,7 +352,8 @@
             sum_top[f] = tops[f]
 
         for f in range(2):
-            target = send_y.at[f, h].reshape(1024, LANES)
+            target, size = (send_pair.reshape(2048, LANES), 8) if h == 0 else (send_y.at[f].reshape(1024, LANES), 4)
+            start = 4 * f if h == 0 else 0
 
             def sum_x(p, _):
                 both = []
@@ -362,32 +374,38 @@
                     )
                 result = table_times(table("x_first_t"), jnp.concatenate(both, axis=1))
                 for e in range(2):
-                    target[pl.ds(2 * p + e, XA, stride=4), :] = result[:, e * LANES:(e + 1) * LANES]
+                    target[pl.ds(start + 2 * p + e, XA, stride=size), :] = result[:, e * LANES:(e + 1) * LANES]
                 return 0
 
             lax.fori_loop(0, 2, sum_x, 0, unroll=True)
-            arrived_y[f, h] = exchange(
-                send_y.at[f, h], recv_y.at[f, h], sends.at[3 + 2 * f + h], recv_sem_y.at[2 * f + h],
-                local_sem.at[6 + 2 * f + h],
-            )
+            if h == 1:
+                arrived_y[f] = exchange(
+                    send_y.at[f], recv_y.at[f], sends.at[4 + f], recv_sem_y.at[1 + f], local_sem.at[7 + f]
+                )
+        if h == 0:
+            arrived_pair = exchange(send_pair, recv_pair, sends.at[3], recv_sem_y.at[0], local_sem.at[6])
 
     for f in range(2):
-        for h in range(2):
-            arrived_y[f, h]()
+        if f == 0:
+            arrived_pair()
+        arrived_y[f]()
+        name = ("y_cos", "y_sin")[f]
 
         def sum_y(g, _):
             at = pl.multiple_of(g * LANES, LANES)
             half = pl.ds(pl.multiple_of(g * 64, 64), 64)
-            value = jnp.concatenate([recv_y.at[f, h].reshape(1024, LANES)[half, :] for h in range(2)], axis=0).T
-            result = times_table(value, table(("y_cos", "y_sin")[f]))
+            low = recv_pair.reshape(2048, LANES)[pl.ds(at, LANES), :].T
+            high = recv_y.at[f].reshape(1024, LANES)[half, :].T
+            result = times_table(low, table(name)) + times_table(high, table(name + "_rest"))
             bc[pl.ds(at, LANES), :] = result[:, :LANES]
             bs[pl.ds(at, LANES), :] = result[:, LANES:]
 
             @pl.when(g == 0)
             def _():
-                result = times_table(value[:32], table(("y_cos_top", "y_sin_top")[f]))
-                bc[:32, :] = result[:, :LANES]
-                bs[:32, :] = result[:, LANES:]
+                top = times_table(low[:32], table(name + "_top"))
+                top = top + times_table(high[:32], table(name + "_top_rest"))
+                bc[:32, :] = top[:, :LANES]
+                bs[:32, :] = top[:, LANES:]
 
             return 0
 
@@ -467,8 +485,10 @@
             pltpu.VMEM((1024, LANES), F32),
             pltpu.VMEM((8, 2 * LANES), F32),
             pltpu.VMEM((2, 8, 2 * LANES), F32),
-            pltpu.VMEM((2, 2, DEVICES, 4, LANES), F32),
-            pltpu.VMEM((2, 2, DEVICES, 4, LANES), F32),
+            pltpu.VMEM((DEVICES, 8, LANES), F32),
+            pltpu.VMEM((DEVICES, 8, LANES), F32),
+            pltpu.VMEM((2, DEVICES, 4, LANES), F32),
+            pltpu.VMEM((2, DEVICES, 4, LANES), F32),
             pltpu.VMEM((2,) + flat, F32),
             pltpu.SemaphoreType.DMA((4,)),
             pltpu.SemaphoreType.DMA((18,)),

time: 154 us -> 154 us (level)
  no operation moved by 1% of the time
where the time goes in v5:
time: 154 us
  Pallas kernels  154 us (100%)
    pallas_call x1, Pallas kernels, on_device(): pl.pallas_call(kernel, out_shape=[jax.ShapeDtypeStruct(flat, F32)] * 2, i...  152 us

profile of v5, /device:TPU:1, one launch (start us, length us, event | category | flops | bytes accessed | tf_op | source)
XLA Modules:
  0.0 154.3 jit_solution(4040219363806713221)
XLA Ops:
  0.6 152.2 %field.1 = (f32[2048,128]{1,0:T(8,128)S(1)}, f32[2048,128]{1,0:T(8,128)S(1)}) custom-call(s32[256,1024]{1,0:T(8,128)} %counts_hbm.1, f32[256,1024]{1,0:T(8,128)} %inverse_hbm.1, f32[5824,128]{1,0:T(8,128)} %constant.4.clone.products_hbm, f32[896,128]{1,0:T(8,128)} %constant.5.clone.singles_hbm), custom_call_target="tpu_custom_call" | custom-call | tf_op jit(solution)/shard_map/field/pallas_call | solution.py:465
  152.8 1.3 settle.1
